TPU v7x, 128 devices: a whole 4x4x4 slice. The times are simulated.
128 devices in a mesh: group: 4 (over y), member: 32 (over x, z, core).
Axes of the slice: x: 4, y: 4, z: 4, core: 2. Of those that a mesh axis runs over, the one named last changes fastest.
Arguments:
- values: bfloat16 [4096, 16, 128, 128], P(('group', 'member')), may hold values from -6 to 6
- block_ids: int32 [4096, 16], P(('group', 'member')), may hold values from 0 to 4095, as said below
- target: float32 [4096, 128], P(('group', 'member')), may hold values from -6 to 6
- table: bfloat16 [4096, 128, 256], P(('group', 'member')), may hold values from -0.03125 to 0.03125
- linear: bfloat16 [4096, 128], P(('group', 'member')), may hold values from -0.125 to 0.125
- block_class: int32 [4096], P(('group', 'member')), may hold values from 0 to 256, as said below
Outputs:
- emb_grad: float32 [4096, 128, 256], P(('group', 'member'))
- lin_grad: float32 [4096, 128], P(('group', 'member'))
- residual: float32 [4096, 128], P(('group', 'member'))
Inputs may be any that keep to these rules, and one draw needn't show every extreme that they name: `block_ids`: each tile's 16 blocks have 16 different owners, the owner of block b being b // 32; all blocks of one owner named in the tiles of one device are the same block. `block_class`: each value is 0, 64 or 256.
All inputs are finite; a program needn't handle non-finite values.
Results may differ from a plain program's by a relative error of at most 0.0043.
Values may be sent and summed in bfloat16 or wider, within the bound.
No kernel may reach another device: no remote copies, remote signals or barrier semaphores. Data moves between devices by JAX's collectives and lax.ppermute only.
A program may use at most 192 MiB of HBM per device.

v0:
```python
import jax
import jax.numpy as jnp
from jax import lax
from jax.sharding import PartitionSpec as P


def send_rows(emb_rows, lin_rows):
    return (
        lax.all_to_all(emb_rows, ("group", "member"), split_axis=0, concat_axis=0, tiled=True),
        lax.all_to_all(lin_rows, ("group", "member"), split_axis=0, concat_axis=0, tiled=True),
    )


def send_grads(acc_emb, acc_lin):
    return (
        lax.all_to_all(acc_emb, ("group", "member"), split_axis=0, concat_axis=0, tiled=True),
        lax.all_to_all(acc_lin, ("group", "member"), split_axis=0, concat_axis=0, tiled=True),
    )


def on_device(values, block_ids, target, table, linear, block_class):
    groups = lax.axis_size("group")
    members = lax.axis_size("member")
    peers = groups * members
    blk_dev = table.shape[0]
    brows = table.shape[1]
    emb_cols = table.shape[2]
    tiles_dev = values.shape[0]
    per_tile = values.shape[1]
    tsamp = values.shape[2]
    gscale = (tsamp * tiles_dev * per_tile / blk_dev) ** (-0.5)
    owners = block_ids // blk_dev
    local_index = block_ids % blk_dev
    matches = owners.reshape(-1)[:, None] == jnp.arange(peers, dtype=jnp.int32)[None, :]
    wanted = jnp.max(jnp.where(matches, local_index.reshape(-1)[:, None], -1), axis=0)
    request = jnp.maximum(wanted, 0).reshape(peers, 1)
    col_mask = jnp.arange(emb_cols)[None, :] < block_class[:, None]
    factors = jnp.where(col_mask[:, None, :], table, jnp.zeros_like(table))
    received = lax.all_to_all(request, ("group", "member"), split_axis=0, concat_axis=0, tiled=True)
    emb_rows = factors[received]
    lin_rows = linear[received]
    back_emb, back_lin = send_rows(emb_rows, lin_rows)
    pulled_emb = back_emb
    pulled_lin = back_lin
    pulled_emb = pulled_emb.reshape(peers, brows, emb_cols)
    pulled_lin = pulled_lin.reshape(peers, brows)

    def one_tile(carry, inputs):
        acc_emb, acc_lin = carry
        tile_vals, tile_owner, tile_target = inputs
        picked = pulled_emb[tile_owner]
        picked_lin = pulled_lin[tile_owner]
        vals_f = tile_vals.astype(jnp.float32)
        sq_vals = (vals_f * vals_f).astype(jnp.bfloat16)
        picked_f = picked.astype(jnp.float32)
        sq_fac = (picked_f * picked_f).astype(jnp.bfloat16)
        sums = jnp.einsum("ksf,kfd->sd", tile_vals, picked, preferred_element_type=jnp.float32)
        squares = jnp.einsum("ksf,kfd->sd", sq_vals, sq_fac, preferred_element_type=jnp.float32)
        lin_part = jnp.einsum(
            "ksf,kf->s", tile_vals, picked_lin, preferred_element_type=jnp.float32
        )
        resid = lin_part + 0.5 * jnp.sum(sums * sums - squares, axis=1) - tile_target
        scaled = resid * gscale
        scaled_b = scaled.astype(jnp.bfloat16)
        weighted = (scaled[:, None] * sums).astype(jnp.bfloat16)
        term = jnp.einsum("ksf,sd->kfd", tile_vals, weighted, preferred_element_type=jnp.float32)
        decay_factor = jnp.einsum(
            "ksf,s->kf", sq_vals, scaled_b, preferred_element_type=jnp.float32
        )
        term = term - decay_factor[:, :, None] * picked_f
        lin_term = jnp.einsum("ksf,s->kf", tile_vals, scaled_b, preferred_element_type=jnp.float32)
        acc_emb = acc_emb.at[tile_owner].add(term)
        acc_lin = acc_lin.at[tile_owner].add(lin_term)
        return ((acc_emb, acc_lin), resid)

    start = (
        jnp.zeros((peers, brows, emb_cols), jnp.float32),
        jnp.zeros((peers, brows), jnp.float32),
    )
    (acc_emb, acc_lin), residual = lax.scan(one_tile, start, (values, owners, target))
    recv_emb, incoming_linear = send_grads(acc_emb, acc_lin)
    asked_idx = received.reshape(peers)
    onehot = (jnp.arange(blk_dev, dtype=jnp.int32)[:, None] == asked_idx[None, :]).astype(
        jnp.float32
    )
    emb_grad = jnp.einsum("bp,pfd->bfd", onehot, recv_emb, precision=lax.Precision.HIGHEST)
    emb_grad = emb_grad * col_mask[:, None, :].astype(jnp.float32)
    lin_grad = jnp.dot(onehot, incoming_linear, precision=lax.Precision.HIGHEST)
    return (emb_grad, lin_grad, residual)


def solution(mesh):
    return jax.shard_map(
        on_device,
        mesh=mesh,
        in_specs=(
            P(("group", "member"), None, None, None),
            P(("group", "member"), None),
            P(("group", "member"), None),
            P(("group", "member"), None, None),
            P(("group", "member"), None),
            P(("group", "member")),
        ),
        out_specs=(
            P(("group", "member"), None, None),
            P(("group", "member"), None),
            P(("group", "member"), None),
        ),
        check_vma=False,
    )
```

profile of v0, /device:TPU:66, one launch (start us, length us, event | category | flops | bytes accessed | tf_op | source)
XLA Modules:
  0.0 1068.2 jit_solution(6039173513890547029)
XLA Ops:
  2.6 10.0 all-to-all-start
  13.4 6.0 all-to-all-done
  19.3 4.7 fusion.49
  25.4 7.3 all-to-all-start.1
  34.5 6.6 gather_fusion.3
  41.1 10.2 all-to-all-start.2
  51.3 99.9 %all-to-all-done.2 = bf16[128,1,128,256]{3,2,1,0:T(8,128)(2,1)} async-done(((bf16[128,1,128,256]{3,2,1,0:T(8,128)(2,1)}), bf16[128,1,128,256]{3,2,1,0:T(8,128)(2,1)}, u32[]{:S(2)}, u32[]{:S(2)}) %all-to-all-start.2) | async-done | bytes 8388640 | tf_op jit(solution)/shard_map/all_to_all | solution.py:9
  151.2 7.8 broadcast_in_dim.55
  159.0 623.6 %while.14 = (s32[]{:T(128)}, f32[128,128,256]{2,1,0:T(8,128)}, f32[128,128]{1,0:T(8,128)S(1)}, f32[32,128]{1,0:T(8,128)}, s32[32,16]{1,0:T(8,128)S(1)}, /*index=...) while((s32[]{:T(128)}, f32[128,128,256]{2,1,0:T(8,128)}, ...), condition=%wide.region_5.6_spmd, body=%wide.region_1.5_spmd.sunk | while | flops 409636800 | bytes 17242704 | solution.py:80
  212.9 4.7 scatter_fusion
  290.8 4.6 scatter_fusion
  310.3 4.6 scatter_fusion
  329.8 4.6 scatter_fusion
  407.7 4.7 scatter_fusion
  427.2 4.6 scatter_fusion
  446.7 4.6 scatter_fusion
  583.0 4.7 scatter_fusion
  641.5 4.7 scatter_fusion
  719.4 4.7 scatter_fusion
  758.5 4.6 scatter_fusion
  782.6 16.1 %all_to_all.33 = f32[128,1,128]{2,1,0:T(1,128)S(1)} all-to-all(f32[128,1,128]{2,1,0:T(1,128)S(1)} %bitcast.107), channel_id=1, replica_groups=mesh['group'=4,'member'=32] {'group','member'}, dimensions={0} | all-to-all | bytes 131072 | tf_op jit(solution)/shard_map/all_to_all | solution.py:17
  798.7 8.7 all-to-all-start.3
  808.1 235.2 %all-to-all-done.3 = f32[128,128,256]{2,1,0:T(8,128)} async-done(((f32[128,128,256]{2,1,0:T(8,128)}), f32[128,128,256]{2,1,0:T(8,128)}, u32[]{:S(2)}, u32[]{:S(2)}) %all-to-all-start.3) | async-done | bytes 16777248 | tf_op jit(solution)/shard_map/all_to_all | solution.py:16
  1043.3 20.5 %broadcast_multiply_fusion.3 = f32[32,128,256]{2,0,1:T(8,128)S(1)} fusion(f32[32,256]{1,0:T(8,128)S(1)} %get-tuple-element.95, f32[128,128,256]{2,1,0:T(8,128)} %all-to-all-done.3, s32[128]{0:T(128)S(1)} %get-tuple-element.70), kind=kOutput, calls=%fused_computation.54 | convolution fusion | flops 1611665408 | bytes 21004800 | tf_op jit(solution)/shard_map/bp,pfd->bfd/dot_general | solution.py:86
  (427 shorter events, 582.3 us)
Async XLA Ops:
  0.6 23.4 %copy-start = (bf16[32,128]{1,0:T(8,128)(2,1)S(1)}, bf16[32,128]{1,0:T(8,128)(2,1)}, u32[]{:S(2)}) copy-start(bf16[32,128]{1,0:T(8,128)(2,1)} %param.12) | copy-start | bytes 24580
  2.6 16.7 %all-to-all-start = ((s32[128,1,1]{2,1,0:T(1,128)}), s32[128,1,1]{2,1,0:T(1,128)S(1)}, u32[]{:S(2)}, u32[]{:S(2)}) async-start(s32[128,1,1]{2,1,0:T(1,128)} %copy.46), calls=%async_computation | async-start | bytes 131072 | tf_op jit(solution)/shard_map/all_to_all | solution.py:39
  25.4 15.6 %all-to-all-start.1 = ((bf16[128,1,128]{2,1,0:T(2,128)(2,1)}), bf16[128,1,128]{2,1,0:T(2,128)(2,1)S(1)}, u32[]{:S(2)}, u32[]{:S(2)}) async-start(bf16[128,1,128]{2,1,0:T(2,128)(2,1)} %copy.47), calls=%async_computation.1 | async-start | bytes 131072 | tf_op jit(solution)/shard_map/all_to_all | solution.py:10
  41.1 110.1 %all-to-all-start.2 = ((bf16[128,1,128,256]{3,2,1,0:T(8,128)(2,1)}), bf16[128,1,128,256]{3,2,1,0:T(8,128)(2,1)}, u32[]{:S(2)}, u32[]{:S(2)}) async-start(bf16[128,1,128,256]{3,2,1,0:T(8,128)(2,1)} %bitcast.106), calls=%async_computation.2 | async-start | bytes 16777216 | tf_op jit(solution)/shard_map/all_to_all | solution.py:9
  798.7 244.6 %all-to-all-start.3 = ((f32[128,128,256]{2,1,0:T(8,128)}), f32[128,128,256]{2,1,0:T(8,128)}, u32[]{:S(2)}, u32[]{:S(2)}) async-start(f32[128,128,256]{2,1,0:T(8,128)} %get-tuple-element.52), calls=%async_computation.3 | async-start | bytes 33554432 | tf_op jit(solution)/shard_map/all_to_all | solution.py:16
  1043.3 24.9 %copy-start.1 = (bf16[32,128]{1,0:T(8,128)(2,1)S(1)}, bf16[32,128]{1,0:T(8,128)(2,1)}, u32[]{:S(2)}) copy-start(bf16[32,128]{1,0:T(8,128)(2,1)} %param.12) | copy-start | bytes 24580
where the time goes:
time: 1080 us; the launch traced here: 1070 us
  waiting for transfers between devices  341 us (32%)
  matrix products  286 us (26%)
  local copies, waits for them, and re-layouts  209 us (19%)
  other arithmetic  178 us (16%)
  starting transfers between devices  36.2 us (3%)
  blocking collectives  16.1 us (1%)
    all_to_all x1, waiting for transfers between devices, send_grads(): lax.all_to_all(acc_emb, ('group', 'member'), split_axis=0, concat_axis=0,...  235 us
    scatter-add x32, other arithmetic, one_tile(): acc_emb = acc_emb.at[tile_owner].add(term)  148 us
    gather x32, local copies, waits for them, and re-layouts, one_tile(): picked = pulled_emb[tile_owner]  128 us
    all_to_all x1, waiting for transfers between devices, send_rows(): lax.all_to_all(emb_rows, ('group', 'member'), split_axis=0, concat_axis=0...  99.9 us
    dot_general x32, matrix products, one_tile(): jnp.einsum('ksf,sd->kfd', tile_vals, weighted, preferred_element_type=jnp...  51.8 us
    dot_general x32, matrix products, one_tile(): jnp.einsum('ksf,kfd->sd', sq_vals, sq_fac, preferred_element_type=jnp.flo...  48.5 us
    dot_general x32, matrix products, one_tile(): jnp.einsum('ksf,kfd->sd', tile_vals, picked, preferred_element_type=jnp.f...  43.7 us
    dynamic_update_slice x32, local copies, waits for them, and re-layouts, on_device(): lax.scan(one_tile, start, (values, owners, target))  41.3 us
  transfers between devices with their start and end apart: 4, of which 3 were waited for; matrix products, arithmetic and copies ran while one was open for 1% of the time, Pallas kernels for 0%

commit v1 on v0

v1 whole, which is shorter than its diff:
```python
import jax
import jax.numpy as jnp
from jax import lax
from jax.experimental import pallas as pl
from jax.experimental.pallas import tpu as pltpu
from jax.sharding import PartitionSpec as P

AXES = ("group", "member")
EXTRA = 16
NT = (((1,), (1,)), ((), ()))
NN = (((1,), (0,)), ((), ()))
F32 = jnp.float32
BF16 = jnp.bfloat16


def swap(x):
    return lax.all_to_all(x, AXES, split_axis=0, concat_axis=0, tiled=True)


def prepare_body(cls_ref, table_ref, lin_ref, out_ref):
    step = pl.program_id(0)
    per = table_ref.shape[0]
    brows, cols = table_ref.shape[1:]
    for i in range(per):
        width = cls_ref[step * per + i]
        row = lax.broadcasted_iota(jnp.int32, (cols, brows), 0)
        vt = jnp.where(row < width, table_ref[i].astype(F32).T, 0.0)
        sq = (vt * vt).astype(BF16).astype(F32)
        total = jnp.sum(sq, axis=0, keepdims=True)
        hi = total.astype(BF16).astype(F32)
        mid = (total - hi).astype(BF16).astype(F32)
        low = total - hi - mid
        at = lax.broadcasted_iota(jnp.int32, (EXTRA, brows), 0)
        extra = jnp.where(at == 0, lin_ref[i].astype(F32), 0.0)
        extra = jnp.where(at == 1, hi, extra)
        extra = jnp.where(at == 2, mid, extra)
        extra = jnp.where(at == 3, low, extra)
        out_ref[i, :cols] = vt.astype(BF16)
        out_ref[i, cols:] = extra.astype(BF16)


def prepare(table, linear, block_class):
    blocks, brows, cols = table.shape
    per = 8
    return pl.pallas_call(
        prepare_body,
        grid=(blocks // per,),
        in_specs=[
            pl.BlockSpec(memory_space=pltpu.SMEM),
            pl.BlockSpec((per, brows, cols), lambda i: (i, 0, 0)),
            pl.BlockSpec((per, 1, brows), lambda i: (i, 0, 0)),
        ],
        out_specs=pl.BlockSpec((per, cols + EXTRA, brows), lambda i: (i, 0, 0)),
        out_shape=jax.ShapeDtypeStruct((blocks, cols + EXTRA, brows), BF16),
        cost_estimate=pl.CostEstimate(flops=1 << 24, bytes_accessed=1 << 22, transcendentals=0),
        name="prepare",
    )(block_class, table, linear.reshape(blocks, 1, brows))


def pick_body(idx_ref, rows_ref, out_ref, sem):
    peers = out_ref.shape[0]

    @pl.loop(0, peers)
    def _(p):
        pltpu.make_async_copy(rows_ref.at[idx_ref[p]], out_ref.at[p], sem).start()

    pltpu.make_async_copy(out_ref, out_ref, sem).wait()


def pick(idx, rows):
    peers = idx.shape[0]
    return pl.pallas_call(
        pick_body,
        in_specs=[
            pl.BlockSpec(memory_space=pltpu.SMEM),
            pl.BlockSpec(memory_space=pltpu.VMEM),
        ],
        out_specs=pl.BlockSpec(memory_space=pl.ANY),
        out_shape=jax.ShapeDtypeStruct((peers, *rows.shape[1:]), rows.dtype),
        scratch_shapes=[pltpu.SemaphoreType.DMA],
        name="pick",
    )(idx, rows)


def tiles_body(gscale, own_ref, x_ref, pulled_ref, target_ref, out_ref, resid_ref, acc_ref):
    t = pl.program_id(0)
    steps = pl.num_programs(0)
    per_tile, tsamp, brows = x_ref.shape[1:]
    peers, rows, _ = pulled_ref.shape
    cols = rows - EXTRA

    @pl.when(t == 0)
    def _():
        @pl.loop(0, peers)
        def _(o):
            acc_ref[o] = jnp.zeros((rows, brows), F32)

    sums = jnp.zeros((rows, tsamp), F32)
    squares = jnp.zeros((EXTRA, tsamp), F32)
    for k in range(0, per_tile, 2):
        a, b = own_ref[t, k], own_ref[t, k + 1]
        x = jnp.concatenate([x_ref[0, k], x_ref[0, k + 1]], axis=1)
        v = jnp.concatenate([pulled_ref[a], pulled_ref[b]], axis=1)
        sums = sums + lax.dot_general(v, x, NT, preferred_element_type=F32)
        squares = squares + lax.dot_general(v[cols:], x * x, NT, preferred_element_type=F32)
    main = sums[:cols]
    square = squares[1:2] + squares[2:3] + squares[3:4]
    inter = jnp.sum(main * main, axis=0, keepdims=True)
    resid = sums[cols : cols + 1] + 0.5 * (inter - square) - target_ref[pl.ds(t, 1), :]
    resid_ref[pl.ds(t, 1), :] = resid
    scaled = resid * gscale
    weighted = (main * scaled).astype(BF16)
    at = lax.broadcasted_iota(jnp.int32, (EXTRA, tsamp), 0)
    lin_lhs = jnp.where(at == 0, scaled, 0.0).astype(BF16)
    sq_lhs = jnp.where(at == 1, scaled, 0.0).astype(BF16)
    for k in range(0, per_tile, 2):
        a, b = own_ref[t, k], own_ref[t, k + 1]
        x = jnp.concatenate([x_ref[0, k], x_ref[0, k + 1]], axis=1)
        term = lax.dot_general(weighted, x, NN, preferred_element_type=F32)
        rest = lax.dot_general(lin_lhs, x, NN, preferred_element_type=F32)
        rest = rest + lax.dot_general(sq_lhs, x * x, NN, preferred_element_type=F32)
        for o, part in ((a, slice(0, brows)), (b, slice(brows, 2 * brows))):
            acc_ref[o, :cols] += term[:, part]
            acc_ref[o, cols:] += rest[:, part]

    @pl.when(t == steps - 1)
    def _():
        @pl.loop(0, peers)
        def _(o):
            out_ref[o, :cols] = acc_ref[o, :cols].astype(BF16)
            extra = acc_ref[o, cols:]
            hi = extra.astype(BF16).astype(F32)
            out_ref[o, cols:] = (hi + pltpu.roll(extra - hi, 2, 0)).astype(BF16)


def tiles(owners, values, pulled, target, gscale):
    n_tiles, per_tile, tsamp, brows = values.shape
    peers, rows, _ = pulled.shape
    return pl.pallas_call(
        lambda *refs: tiles_body(gscale, *refs),
        grid=(n_tiles,),
        in_specs=[
            pl.BlockSpec(memory_space=pltpu.SMEM),
            pl.BlockSpec((1, per_tile, tsamp, brows), lambda t: (t, 0, 0, 0)),
            pl.BlockSpec(memory_space=pltpu.VMEM),
            pl.BlockSpec(memory_space=pltpu.VMEM),
        ],
        out_specs=[
            pl.BlockSpec(memory_space=pltpu.VMEM),
            pl.BlockSpec(memory_space=pltpu.VMEM),
        ],
        out_shape=[
            jax.ShapeDtypeStruct((peers, rows, brows), BF16),
            jax.ShapeDtypeStruct((n_tiles, tsamp), F32),
        ],
        scratch_shapes=[pltpu.VMEM((peers, rows, brows), F32)],
        compiler_params=pltpu.CompilerParams(vmem_limit_bytes=60 << 20),
        name="tiles",
    )(owners, values, pulled, target)


def reduce_body(idx_ref, cls_ref, recv_ref, rows_ref, emb_ref, lin_ref, acc_ref):
    step = pl.program_id(0)
    per = recv_ref.shape[0]
    blocks, rows, brows = acc_ref.shape
    cols = rows - EXTRA

    @pl.when(step == 0)
    def _():
        @pl.loop(0, blocks)
        def _(j):
            acc_ref[j] = jnp.zeros((rows, brows), F32)

    for i in range(per):
        j = idx_ref[step * per + i]
        acc_ref[j] += recv_ref[i].astype(F32)

    @pl.when(step == pl.num_programs(0) - 1)
    def _():
        @pl.loop(0, blocks)
        def _(j):
            extra = acc_ref[j, cols:]
            lin_ref[pl.ds(j, 1), :] = extra[0:1] + extra[2:3]
            decay = extra[1:2] + extra[3:4]
            grad = acc_ref[j, :cols] - decay * rows_ref[j, :cols].astype(F32)
            row = lax.broadcasted_iota(jnp.int32, (cols, brows), 0)
            emb_ref[j] = jnp.where(row < cls_ref[j], grad, 0.0).T


def reduce_grads(idx, block_class, recv, rows_t):
    peers, rows, brows = recv.shape
    blocks = block_class.shape[0]
    cols = rows - EXTRA
    per = 16
    return pl.pallas_call(
        reduce_body,
        grid=(peers // per,),
        in_specs=[
            pl.BlockSpec(memory_space=pltpu.SMEM),
            pl.BlockSpec(memory_space=pltpu.SMEM),
            pl.BlockSpec((per, rows, brows), lambda i: (i, 0, 0)),
            pl.BlockSpec(memory_space=pltpu.VMEM),
        ],
        out_specs=[
            pl.BlockSpec(memory_space=pltpu.VMEM),
            pl.BlockSpec(memory_space=pltpu.VMEM),
        ],
        out_shape=[
            jax.ShapeDtypeStruct((blocks, brows, cols), F32),
            jax.ShapeDtypeStruct((blocks, brows), F32),
        ],
        scratch_shapes=[pltpu.VMEM((blocks, rows, brows), F32)],
        compiler_params=pltpu.CompilerParams(vmem_limit_bytes=40 << 20),
        name="reduce_grads",
    )(idx, block_class, recv, rows_t)


def on_device(values, block_ids, target, table, linear, block_class):
    peers = lax.axis_size("group") * lax.axis_size("member")
    blk_dev = table.shape[0]
    n_tiles, per_tile, tsamp, _ = values.shape
    gscale = (tsamp * n_tiles * per_tile / blk_dev) ** (-0.5)
    owners = block_ids // blk_dev
    local_index = block_ids % blk_dev
    matches = owners.reshape(-1)[:, None] == jnp.arange(peers, dtype=jnp.int32)[None, :]
    wanted = jnp.max(jnp.where(matches, local_index.reshape(-1)[:, None], 0), axis=0)
    idx = swap(wanted.reshape(peers, 1)).reshape(peers)
    rows_t = prepare(table, linear, block_class)
    pulled = swap(pick(idx, rows_t))
    acc, residual = tiles(owners, values, pulled, target, gscale)
    recv = swap(acc)
    emb_grad, lin_grad = reduce_grads(idx, block_class, recv, rows_t)
    return emb_grad, lin_grad, residual


def solution(mesh):
    return jax.shard_map(
        on_device,
        mesh=mesh,
        in_specs=(
            P(AXES, None, None, None),
            P(AXES, None),
            P(AXES, None),
            P(AXES, None, None),
            P(AXES, None),
            P(AXES),
        ),
        out_specs=(P(AXES, None, None), P(AXES, None), P(AXES, None)),
        check_vma=False,
    )
```

time: 1080 us -> 320 us (0.30)
  waiting for transfers between devices: 341 us -> 0.96 us
  matrix products: 286 us -> 0 us
  local copies, waits for them, and re-layouts: 209 us -> 3 us
  blocking collectives: 16.1 us -> 220 us
  other arithmetic: 178 us -> 3.18 us
  Pallas kernels: 0 us -> 77.2 us
  starting transfers between devices: 36.2 us -> 10 us
    all_to_all x4 -> x1, waiting for transfers between devices: 341 us -> 0.96 us  [swap(): return lax.all_to_all(x, AXES, split_axis=0, concat_axis=0, tiled=True)]
    dot_general x194 -> x0, matrix products: 286 us -> none  [the longest x32 51.8 us: one_tile(): jnp.einsum('ksf,sd->kfd', tile_vals, weighted, preferred_element_type=jnp...]
    all_to_all x1 -> x2, blocking collectives: 16.1 us -> 220 us  [swap(): return lax.all_to_all(x, AXES, split_axis=0, concat_axis=0, tiled=True)]
    scatter-add x64 -> x0, other arithmetic: 170 us -> none  [the longest x32 148 us: one_tile(): acc_emb = acc_emb.at[tile_owner].add(term)]
    gather x67 -> x0, local copies, waits for them, and re-layouts: 154 us -> none  [the longest x32 128 us: one_tile(): picked = pulled_emb[tile_owner]]
    pallas_call x0 -> x4, Pallas kernels: none -> 77.2 us  [the longest x1 59.1 us: tiles(): pl.pallas_call(lambda *refs: tiles_body(gscale, *refs), grid=(n_tiles,),...]
    dynamic_update_slice x32 -> x0, local copies, waits for them, and re-layouts: 41.3 us -> none  [on_device(): lax.scan(one_tile, start, (values, owners, target))]
    all_to_all x4 -> x1, starting transfers between devices: 36.2 us -> 10 us  [swap(): return lax.all_to_all(x, AXES, split_axis=0, concat_axis=0, tiled=True)]
  transfers between devices with their start and end apart: 4 -> 1, of which waited for: 3 -> 1; matrix products, arithmetic and copies ran while one was open for 1% -> 0% of each run, Pallas kernels for 0% -> 1%
where the time goes in v1:
time: 320 us; the launch traced here: 315 us
  blocking collectives  220 us (69%)
  Pallas kernels  77.2 us (24%)
  starting transfers between devices  10 us (3%)
    all_to_all x2, blocking collectives, swap(): return lax.all_to_all(x, AXES, split_axis=0, concat_axis=0, tiled=True)  220 us
    pallas_call x1, Pallas kernels, tiles(): pl.pallas_call(lambda *refs: tiles_body(gscale, *refs), grid=(n_tiles,),...  59.1 us
    all_to_all x1, starting transfers between devices, swap(): return lax.all_to_all(x, AXES, split_axis=0, concat_axis=0, tiled=True)  10 us
    pallas_call x1, Pallas kernels, reduce_grads(): pl.pallas_call(reduce_body, grid=(peers // per,), in_specs=[pl.BlockSpec(...  8.42 us
  transfers between devices with their start and end apart: 1, of which 1 were waited for; matrix products, arithmetic and copies ran while one was open for 0% of the time, Pallas kernels for 1%

profile of v1, /device:TPU:66, one launch (start us, length us, event | category | flops | bytes accessed | tf_op | source)
XLA Modules:
  0.0 314.9 jit_solution(8569473238719166264)
XLA Ops:
  0.6 0.8 copy.30
  1.4 0.0 copy-start.3
  1.4 0.1 broadcast_in_dim.15
  1.5 0.1 eq.17
  1.6 0.2 select_reduce_fusion
  1.8 0.7 copy.34
  2.6 10.0 %all-to-all-start = ((s32[128,1,1]{2,1,0:T(1,128)}), s32[128,1,1]{2,1,0:T(1,128)S(1)}, u32[]{:S(2)}, u32[]{:S(2)}) async-start(s32[128,1,1]{2,1,0:T(1,128)} %copy.34), calls=%async_computation | async-start | bytes 131072 | tf_op jit(solution)/shard_map/all_to_all | solution.py:17
  12.6 1.3 copy.35.lin_ref
  13.9 4.5 %prepare.1.rows_ref = bf16[32,272,128]{2,1,0:T(8,128)(2,1)} custom-call(s32[32]{0:T(128)} %cls_ref.3, bf16[32,128,256]{2,1,0:T(8,128)(2,1)} %table_ref.1, bf16[32,1,128]{2,1,0:T(2,128)(2,1)} %copy.35.lin_ref), custom_call_target="tpu_custom_call" | custom-call | flops 16777216 | bytes 4194304 | tf_op jit(solution)/shard_map/prepare/pallas_call | solution.py:45
  18.4 1.0 all-to-all-done
  19.4 2.9 reduce.idx_ref
  22.3 5.1 %pick.1 = bf16[128,272,128]{2,1,0:T(8,128)(2,1)} custom-call(s32[128]{0:T(128)} %reduce.idx_ref, bf16[32,272,128]{2,1,0:T(8,128)(2,1)} %prepare.1.rows_ref), custom_call_target="tpu_custom_call" | custom-call | tf_op jit(solution)/shard_map/pick/pallas_call | solution.py:72
  27.4 109.7 %all_to_all.19.refs_2_ = bf16[128,272,128]{2,1,0:T(8,128)(2,1)} all-to-all(bf16[128,272,128]{2,1,0:T(8,128)(2,1)} %pick.1), channel_id=1, replica_groups=mesh['group'=4,'member'=32] {'group','member'}, dimensions={0} | all-to-all | bytes 17825792 | tf_op jit(solution)/shard_map/all_to_all | solution.py:17
  137.1 0.0 copy-done.3
  137.1 59.1 %tiles.1 = (bf16[128,272,128]{2,1,0:T(8,128)(2,1)}, f32[32,128]{1,0:T(8,128)}) custom-call(s32[32,16]{1,0:T(8,128)} %copy-done.3, bf16[32,16,128,128]{3,2,1,0:T(8,128)(2,1)} %refs_1_.1, bf16[128,272,128]{2,1,0:T(8,128)(2,1)} %all_to_all.19.refs_2_, f32[32,128]{1,0:T(8,128)} %refs_3_.1), custom_call_target="tpu_custom_call" | custom-call | tf_op jit(solution)/shard_map/tiles/pallas_call | solution.py:139
  196.3 0.0 copy-start
  196.3 0.0 copy-start.1
  196.3 0.0 copy-start.2
  196.3 110.1 %all_to_all.20.recv_ref = bf16[128,272,128]{2,1,0:T(8,128)(2,1)S(1)} all-to-all(bf16[128,272,128]{2,1,0:T(8,128)(2,1)} %get-tuple-element.7), channel_id=1, replica_groups=mesh['group'=4,'member'=32] {'group','member'}, dimensions={0} | all-to-all | bytes 17825792 | tf_op jit(solution)/shard_map/all_to_all | solution.py:17
  306.4 0.0 copy-done
  306.4 0.0 copy-done.1
  306.4 0.0 copy-done.2
  306.4 8.4 %reduce_grads.1 = (f32[32,128,256]{2,1,0:T(8,128)}, f32[32,128]{1,0:T(8,128)}) custom-call(s32[128]{0:T(128)S(1)} %copy-done.1, s32[32]{0:T(128)S(1)} %copy-done.2, bf16[128,272,128]{2,1,0:T(8,128)(2,1)S(1)} %all_to_all.20.recv_ref, bf16[32,272,128]{2,1,0:T(8,128)(2,1)S(1)} %copy-done), custom_call_target="tpu_custom_call" | custom-call | tf_op jit(solution)/shard_map/reduce_grads/pallas_call | solution.py:195
  (1 shorter events, 0.0 us)
Async XLA Ops:
  1.4 135.7 %copy-start.3 = (s32[32,16]{1,0:T(8,128)}, s32[32,16]{1,0:T(8,128)S(1)}, u32[]{:S(2)}) copy-start(s32[32,16]{1,0:T(8,128)S(1)} %get-tuple-element.11.refs_0_) | copy-start | bytes 6148
  2.6 16.8 %all-to-all-start = ((s32[128,1,1]{2,1,0:T(1,128)}), s32[128,1,1]{2,1,0:T(1,128)S(1)}, u32[]{:S(2)}, u32[]{:S(2)}) async-start(s32[128,1,1]{2,1,0:T(1,128)} %copy.34), calls=%async_computation | async-start | bytes 131072 | tf_op jit(solution)/shard_map/all_to_all | solution.py:17
  196.3 110.2 %copy-start = (bf16[32,272,128]{2,1,0:T(8,128)(2,1)S(1)}, bf16[32,272,128]{2,1,0:T(8,128)(2,1)}, u32[]{:S(2)}) copy-start(bf16[32,272,128]{2,1,0:T(8,128)(2,1)} %prepare.1.rows_ref) | copy-start | bytes 6684676
  196.3 110.2 %copy-start.1 = (s32[128]{0:T(128)S(1)}, s32[128]{0:T(128)}, u32[]{:S(2)}) copy-start(s32[128]{0:T(128)} %reduce.idx_ref) | copy-start | bytes 1540
  196.3 110.2 %copy-start.2 = (s32[32]{0:T(128)S(1)}, s32[32]{0:T(128)}, u32[]{:S(2)}) copy-start(s32[32]{0:T(128)} %cls_ref.3) | copy-start | bytes 388

commit v2 on v1

v2 whole, which is shorter than its diff:
```python
import jax
import jax.numpy as jnp
from jax import lax
from jax.experimental import pallas as pl
from jax.experimental.pallas import tpu as pltpu
from jax.sharding import PartitionSpec as P

AXES = ("group", "member")
EXTRA = 8
NT = (((1,), (1,)), ((), ()))
NN = (((1,), (0,)), ((), ()))
F32 = jnp.float32
BF16 = jnp.bfloat16


def swap(x):
    return lax.all_to_all(x, AXES, split_axis=0, concat_axis=0, tiled=True)


def prepare_body(cls_ref, table_ref, lin_ref, out_ref, lin32_ref):
    blocks, brows, cols = table_ref.shape
    lin32_ref[...] = lin_ref[...].astype(F32)
    one = lax.broadcasted_iota(jnp.int32, (cols, cols), 0)
    one = jnp.where(one == lax.broadcasted_iota(jnp.int32, (cols, cols), 1), 1.0, 0.0).astype(BF16)
    row = lax.broadcasted_iota(jnp.int32, (cols, brows), 0)
    at = lax.broadcasted_iota(jnp.int32, (EXTRA, brows), 0)

    @pl.loop(0, blocks, unroll=4)
    def _(j):
        vt = lax.dot_general(one, table_ref[j], NT, preferred_element_type=F32)
        vt = jnp.where(row < cls_ref[j], vt, 0.0)
        total = jnp.sum((vt * vt).astype(BF16).astype(F32), axis=0, keepdims=True)
        hi = total.astype(BF16).astype(F32)
        mid = (total - hi).astype(BF16).astype(F32)
        low = total - hi - mid
        extra = jnp.where(at == 0, lin32_ref[pl.ds(j, 1), :], 0.0)
        extra = jnp.where(at == 1, hi, extra)
        extra = jnp.where(at == 2, mid, extra)
        extra = jnp.where(at == 3, low, extra)
        out_ref[j] = jnp.concatenate([vt, extra], axis=0).astype(BF16)


def prepare(table, linear, block_class):
    blocks, brows, cols = table.shape
    whole = pl.BlockSpec(memory_space=pltpu.VMEM)
    return pl.pallas_call(
        prepare_body,
        in_specs=[pl.BlockSpec(memory_space=pltpu.SMEM), whole, whole],
        out_specs=whole,
        out_shape=jax.ShapeDtypeStruct((blocks, cols + EXTRA, brows), BF16),
        scratch_shapes=[pltpu.VMEM(linear.shape, F32)],
        compiler_params=pltpu.CompilerParams(vmem_limit_bytes=16 << 20),
        cost_estimate=pl.CostEstimate(flops=1 << 24, bytes_accessed=1 << 22, transcendentals=0),
        name="prepare",
    )(block_class, table, linear)


def pick_body(idx_ref, rows_ref, out_ref):
    @pl.loop(0, out_ref.shape[0], unroll=2)
    def _(p):
        out_ref[p] = rows_ref[idx_ref[p, 0, 0]]


def pick(idx, rows):
    peers = idx.shape[0]
    whole = pl.BlockSpec(memory_space=pltpu.VMEM)
    return pl.pallas_call(
        pick_body,
        in_specs=[pl.BlockSpec(memory_space=pltpu.SMEM), whole],
        out_specs=whole,
        out_shape=jax.ShapeDtypeStruct((peers, *rows.shape[1:]), rows.dtype),
        compiler_params=pltpu.CompilerParams(vmem_limit_bytes=24 << 20),
        name="pick",
    )(idx, rows)


def tiles_body(gscale, own_ref, x_ref, pulled_ref, target_ref, out_ref, resid_ref, acc_ref):
    step = pl.program_id(0)
    per, per_tile, tsamp, brows = x_ref.shape
    peers, rows, _ = pulled_ref.shape
    cols = rows - EXTRA

    @pl.when(step == 0)
    def _():
        @pl.loop(0, peers)
        def _(o):
            acc_ref[o] = jnp.zeros((rows, brows), F32)

    def square(x):
        return (x * x).astype(F32)

    at = lax.broadcasted_iota(jnp.int32, (EXTRA, tsamp), 0)
    left = []
    for i in range(per):
        t = step * per + i
        sums = [jnp.zeros((rows, tsamp), F32)] * 2
        squares = jnp.zeros((tsamp, brows), F32)
        for k in range(0, per_tile, 2):
            n = (k // 2) % 2
            va, vb = pulled_ref[own_ref[t, k]], pulled_ref[own_ref[t, k + 1]]
            xa, xb = x_ref[i, k], x_ref[i, k + 1]
            v = jnp.concatenate([va, vb], axis=1)
            x = jnp.concatenate([xa, xb], axis=1)
            sums[n] += lax.dot_general(v, x, NT, preferred_element_type=F32)
            for vk, xk in ((va, xa), (vb, xb)):
                rest = vk[cols:].astype(F32)
                squares += square(xk) * (rest[1:2] + rest[2:3] + rest[3:4])
        total = sums[0] + sums[1]
        main = total[:cols]
        sub = jnp.sum(squares.T, axis=0, keepdims=True)
        inter = jnp.sum(main * main, axis=0, keepdims=True)
        resid = total[cols : cols + 1] + 0.5 * (inter - sub) - target_ref[pl.ds(t, 1), :]
        resid_ref[pl.ds(t, 1), :] = resid
        scaled = resid * gscale
        lin = jnp.where(at == 0, scaled, 0.0)
        decay = jnp.where(at == 1, scaled, 0.0)
        of_x = jnp.concatenate([main * scaled, lin], axis=0).astype(BF16)
        of_sq = jnp.concatenate([jnp.zeros((cols, tsamp), F32), decay], axis=0).astype(BF16)
        left.append(jnp.concatenate([of_x, of_sq], axis=1))
    for i in range(per):
        t = step * per + i
        for k in range(0, per_tile, 2):
            x = jnp.concatenate([x_ref[i, k], x_ref[i, k + 1]], axis=1)
            both = jnp.concatenate([x, x * x], axis=0)
            term = lax.dot_general(left[i], both, NN, preferred_element_type=F32)
            acc_ref[own_ref[t, k]] += term[:, :brows]
            acc_ref[own_ref[t, k + 1]] += term[:, brows:]

    @pl.when(step == pl.num_programs(0) - 1)
    def _():
        @pl.loop(0, peers)
        def _(o):
            extra = acc_ref[o, cols:]
            hi = extra.astype(BF16).astype(F32)
            extra = hi + pltpu.roll(extra - hi, 2, 0)
            out_ref[o] = jnp.concatenate([acc_ref[o, :cols], extra], axis=0).astype(BF16)


def tiles(owners, values, pulled, target, gscale):
    n_tiles, per_tile, tsamp, brows = values.shape
    peers, rows, _ = pulled.shape
    per = 4
    return pl.pallas_call(
        lambda *refs: tiles_body(gscale, *refs),
        grid=(n_tiles // per,),
        in_specs=[
            pl.BlockSpec(memory_space=pltpu.SMEM),
            pl.BlockSpec((per, per_tile, tsamp, brows), lambda t: (t, 0, 0, 0)),
            pl.BlockSpec(memory_space=pltpu.VMEM),
            pl.BlockSpec(memory_space=pltpu.VMEM),
        ],
        out_specs=[
            pl.BlockSpec(memory_space=pltpu.VMEM),
            pl.BlockSpec(memory_space=pltpu.VMEM),
        ],
        out_shape=[
            jax.ShapeDtypeStruct((peers, rows, brows), BF16),
            jax.ShapeDtypeStruct((n_tiles, tsamp), F32),
        ],
        scratch_shapes=[pltpu.VMEM((peers, rows, brows), F32)],
        compiler_params=pltpu.CompilerParams(vmem_limit_bytes=28 << 20),
        name="tiles",
    )(owners, values, pulled, target)


def reduce_body(idx_ref, cls_ref, recv_ref, rows_ref, emb_ref, lin_ref, acc_ref, done_ref, sem):
    peers = recv_ref.shape[0]
    blocks, rows, brows = acc_ref.shape
    cols = rows - EXTRA

    @pl.loop(0, blocks)
    def _(j):
        acc_ref[j] = jnp.zeros((rows, brows), F32)

    @pl.loop(0, peers, unroll=2)
    def _(p):
        j = idx_ref[p, 0, 0]
        acc_ref[j] += recv_ref[p].astype(F32)

    row = lax.broadcasted_iota(jnp.int32, (cols, brows), 0)

    @pl.loop(0, blocks, unroll=2)
    def _(j):
        extra = acc_ref[j, cols:]
        lin_ref[pl.ds(j, 1), :] = extra[0:1] + extra[2:3]
        decay = extra[1:2] + extra[3:4]
        grad = acc_ref[j, :cols] - decay * rows_ref[j].astype(F32)[:cols]
        done_ref[j] = jnp.where(row < cls_ref[j], grad, 0.0).T
        pltpu.make_async_copy(done_ref.at[j], emb_ref.at[j], sem).start()

    pltpu.make_async_copy(done_ref, emb_ref, sem).wait()


def reduce_grads(idx, block_class, recv, rows_t):
    peers, rows, brows = recv.shape
    blocks = block_class.shape[0]
    cols = rows - EXTRA
    scalars = pl.BlockSpec(memory_space=pltpu.SMEM)
    whole = pl.BlockSpec(memory_space=pltpu.VMEM)
    return pl.pallas_call(
        reduce_body,
        in_specs=[scalars, scalars, whole, whole],
        out_specs=[pl.BlockSpec(memory_space=pl.ANY), whole],
        out_shape=[
            jax.ShapeDtypeStruct((blocks, brows, cols), F32),
            jax.ShapeDtypeStruct((blocks, brows), F32),
        ],
        scratch_shapes=[
            pltpu.VMEM((blocks, rows, brows), F32),
            pltpu.VMEM((blocks, brows, cols), F32),
            pltpu.SemaphoreType.DMA,
        ],
        compiler_params=pltpu.CompilerParams(vmem_limit_bytes=24 << 20),
        name="reduce_grads",
    )(idx, block_class, recv, rows_t)


def on_device(values, block_ids, target, table, linear, block_class):
    peers = lax.axis_size("group") * lax.axis_size("member")
    blk_dev = table.shape[0]
    n_tiles, per_tile, tsamp, _ = values.shape
    gscale = (tsamp * n_tiles * per_tile / blk_dev) ** (-0.5)
    owners = block_ids // blk_dev
    local_index = block_ids % blk_dev
    matches = owners.reshape(-1)[:, None] == jnp.arange(peers, dtype=jnp.int32)[None, :]
    wanted = jnp.max(jnp.where(matches, local_index.reshape(-1)[:, None], 0), axis=0)
    idx = swap(wanted.reshape(peers, 1, 1))
    rows_t = prepare(table, linear, block_class)
    pulled = swap(pick(idx, rows_t))
    acc, residual = tiles(owners, values, pulled, target, gscale)
    recv = swap(acc)
    emb_grad, lin_grad = reduce_grads(idx, block_class, recv, rows_t)
    return emb_grad, lin_grad, residual


def solution(mesh):
    return jax.shard_map(
        on_device,
        mesh=mesh,
        in_specs=(
            P(AXES, None, None, None),
            P(AXES, None),
            P(AXES, None),
            P(AXES, None, None),
            P(AXES, None),
            P(AXES),
        ),
        out_specs=(P(AXES, None, None), P(AXES, None), P(AXES, None)),
        check_vma=False,
    )
```

time: 320 us -> 279 us (0.87)
  Pallas kernels: 77.2 us -> 43.4 us
  blocking collectives: 220 us -> 214 us
    pallas_call x3, Pallas kernels: 72.1 us -> 40.8 us  [the longest x1 30.3 us: tiles(): pl.pallas_call(lambda *refs: tiles_body(gscale, *refs), grid=(n_tiles //...]
    all_to_all x2, blocking collectives: 220 us -> 214 us  [swap(): return lax.all_to_all(x, AXES, split_axis=0, concat_axis=0, tiled=True)]
where the time goes in v2:
time: 279 us; the launch traced here: 274 us
  blocking collectives  214 us (77%)
  Pallas kernels  43.4 us (16%)
  starting transfers between devices  10 us (4%)
  local copies, waits for them, and re-layouts  4.62 us (2%)
    all_to_all x2, blocking collectives, swap(): return lax.all_to_all(x, AXES, split_axis=0, concat_axis=0, tiled=True)  214 us
    pallas_call x1, Pallas kernels, tiles(): pl.pallas_call(lambda *refs: tiles_body(gscale, *refs), grid=(n_tiles //...  30.3 us
    all_to_all x1, starting transfers between devices, swap(): return lax.all_to_all(x, AXES, split_axis=0, concat_axis=0, tiled=True)  10 us
    pallas_call x1, Pallas kernels, reduce_grads(): pl.pallas_call(reduce_body, in_specs=[scalars, scalars, whole, whole], ou...  7.41 us
  transfers between devices with their start and end apart: 1, of which 1 were waited for; matrix products, arithmetic and copies ran while one was open for 0% of the time, Pallas kernels for 1%

profile of v2, /device:TPU:66, one launch (start us, length us, event | category | flops | bytes accessed | tf_op | source)
XLA Modules:
  0.0 274.0 jit_solution(6439959483302207528)
XLA Ops:
  0.6 0.8 copy.19
  1.4 0.1 broadcast_in_dim.15
  1.5 0.1 eq.17
  1.6 0.2 select_reduce_fusion
  1.8 0.7 copy.23
  2.6 10.0 %all-to-all-start = ((s32[128,1,1]{2,1,0:T(1,128)}), s32[128,1,1]{2,1,0:T(1,128)S(1)}, u32[]{:S(2)}, u32[]{:S(2)}) async-start(s32[128,1,1]{2,1,0:T(1,128)} %copy.23), calls=%async_computation | async-start | bytes 131072 | tf_op jit(solution)/shard_map/all_to_all | solution.py:17
  12.6 0.0 copy-start
  12.6 1.6 copy-done
  14.2 0.0 copy-start.2
  14.2 0.7 copy-done.2
  14.9 0.0 copy-start.3
  14.9 0.7 copy-done.3
  15.5 3.1 %prepare.1.rows_ref = bf16[32,264,128]{2,1,0:T(8,128)(2,1)S(1)} custom-call(s32[32]{0:T(128)S(1)} %copy-done.3, bf16[32,128,256]{2,1,0:T(8,128)(2,1)S(1)} %copy-done, bf16[32,128]{1,0:T(8,128)(2,1)S(1)} %copy-done.2), custom_call_target="tpu_custom_call" | custom-call | flops 16777216 | bytes 4194304 | tf_op jit(solution)/shard_map/prepare/pallas_call | solution.py:46
  18.7 0.7 all-to-all-done.idx_ref
  19.3 2.6 pick.1
  21.9 0.0 copy-start.1
  21.9 107.2 %all_to_all.15.refs_2_ = bf16[128,264,128]{2,1,0:T(8,128)(2,1)S(1)} all-to-all(bf16[128,264,128]{2,1,0:T(8,128)(2,1)S(1)} %pick.1), channel_id=1, replica_groups=mesh['group'=4,'member'=32] {'group','member'}, dimensions={0} | all-to-all | bytes 17301504 | tf_op jit(solution)/shard_map/all_to_all | solution.py:17
  129.1 0.0 copy-done.1
  129.1 30.3 %tiles.1 = (bf16[128,264,128]{2,1,0:T(8,128)(2,1)S(1)}, f32[32,128]{1,0:T(8,128)}) custom-call(s32[32,16]{1,0:T(8,128)S(1)} %get-tuple-element.11.refs_0_, bf16[32,16,128,128]{3,2,1,0:T(8,128)(2,1)} %refs_1_.1, bf16[128,264,128]{2,1,0:T(8,128)(2,1)S(1)} %all_to_all.15.refs_2_, f32[32,128]{1,0:T(8,128)S(1)} %copy-done.1), custom_call_target="tpu_custom_call" | custom-call | tf_op jit(solution)/shard_map/tiles/pallas_call | solution.py:143
  159.4 0.0 copy-start.4
  159.4 107.3 %all_to_all.16.recv_ref = bf16[128,264,128]{2,1,0:T(8,128)(2,1)S(1)} all-to-all(bf16[128,264,128]{2,1,0:T(8,128)(2,1)S(1)} %get-tuple-element.7), channel_id=1, replica_groups=mesh['group'=4,'member'=32] {'group','member'}, dimensions={0} | all-to-all | bytes 17301504 | tf_op jit(solution)/shard_map/all_to_all | solution.py:17
  266.6 0.0 copy-done.4
  266.6 7.4 %reduce_grads.1 = (f32[32,128,256]{2,1,0:T(8,128)}, f32[32,128]{1,0:T(8,128)}) custom-call(s32[128,1,1]{2,1,0:T(1,128)S(1)} %all-to-all-done.idx_ref, s32[32]{0:T(128)S(1)} %copy-done.4, bf16[128,264,128]{2,1,0:T(8,128)(2,1)S(1)} %all_to_all.16.recv_ref, bf16[32,264,128]{2,1,0:T(8,128)(2,1)S(1)} %prepare.1.rows_ref), custom_call_target="tpu_custom_call" | custom-call | tf_op jit(solution)/shard_map/reduce_grads/pallas_call | solution.py:200
  (1 shorter events, 0.0 us)
Async XLA Ops:
  2.6 16.7 %all-to-all-start = ((s32[128,1,1]{2,1,0:T(1,128)}), s32[128,1,1]{2,1,0:T(1,128)S(1)}, u32[]{:S(2)}, u32[]{:S(2)}) async-start(s32[128,1,1]{2,1,0:T(1,128)} %copy.23), calls=%async_computation | async-start | bytes 131072 | tf_op jit(solution)/shard_map/all_to_all | solution.py:17
  12.6 1.6 copy-start
  14.2 0.7 copy-start.2
  14.9 0.7 copy-start.3
  21.9 107.2 %copy-start.1 = (f32[32,128]{1,0:T(8,128)S(1)}, f32[32,128]{1,0:T(8,128)}, u32[]{:S(2)}) copy-start(f32[32,128]{1,0:T(8,128)} %refs_3_.1) | copy-start | bytes 49156
  159.4 107.3 %copy-start.4 = (s32[32]{0:T(128)S(1)}, s32[32]{0:T(128)}, u32[]{:S(2)}) copy-start(s32[32]{0:T(128)} %cls_ref.3) | copy-start | bytes 388

commit v3 on v2

--- a/solution.py
+++ b/solution.py
@@ -55,10 +55,12 @@
     )(block_class, table, linear)
 
 
-def pick_body(idx_ref, rows_ref, out_ref):
-    @pl.loop(0, out_ref.shape[0], unroll=2)
+def pick_body(idx_ref, rows_ref, out_ref, flat_ref):
+    @pl.loop(0, out_ref.shape[0], unroll=4)
     def _(p):
-        out_ref[p] = rows_ref[idx_ref[p, 0, 0]]
+        j = idx_ref[p][0, 0]
+        flat_ref[p] = j
+        out_ref[p] = rows_ref[j]
 
 
 def pick(idx, rows):
@@ -66,9 +68,12 @@
     whole = pl.BlockSpec(memory_space=pltpu.VMEM)
     return pl.pallas_call(
         pick_body,
-        in_specs=[pl.BlockSpec(memory_space=pltpu.SMEM), whole],
-        out_specs=whole,
-        out_shape=jax.ShapeDtypeStruct((peers, *rows.shape[1:]), rows.dtype),
+        in_specs=[whole, whole],
+        out_specs=[whole, pl.BlockSpec(memory_space=pltpu.SMEM)],
+        out_shape=[
+            jax.ShapeDtypeStruct((peers, *rows.shape[1:]), rows.dtype),
+            jax.ShapeDtypeStruct((peers,), jnp.int32),
+        ],
         compiler_params=pltpu.CompilerParams(vmem_limit_bytes=24 << 20),
         name="pick",
     )(idx, rows)
@@ -97,7 +102,7 @@
         squares = jnp.zeros((tsamp, brows), F32)
         for k in range(0, per_tile, 2):
             n = (k // 2) % 2
-            va, vb = pulled_ref[own_ref[t, k]], pulled_ref[own_ref[t, k + 1]]
+            va, vb = pulled_ref[own_ref[k, t]], pulled_ref[own_ref[k + 1, t]]
             xa, xb = x_ref[i, k], x_ref[i, k + 1]
             v = jnp.concatenate([va, vb], axis=1)
             x = jnp.concatenate([xa, xb], axis=1)
@@ -123,8 +128,8 @@
             x = jnp.concatenate([x_ref[i, k], x_ref[i, k + 1]], axis=1)
             both = jnp.concatenate([x, x * x], axis=0)
             term = lax.dot_general(left[i], both, NN, preferred_element_type=F32)
-            acc_ref[own_ref[t, k]] += term[:, :brows]
-            acc_ref[own_ref[t, k + 1]] += term[:, brows:]
+            acc_ref[own_ref[k, t]] += term[:, :brows]
+            acc_ref[own_ref[k + 1, t]] += term[:, brows:]
 
     @pl.when(step == pl.num_programs(0) - 1)
     def _():
@@ -174,7 +179,7 @@
 
     @pl.loop(0, peers, unroll=2)
     def _(p):
-        j = idx_ref[p, 0, 0]
+        j = idx_ref[p]
         acc_ref[j] += recv_ref[p].astype(F32)
 
     row = lax.broadcasted_iota(jnp.int32, (cols, brows), 0)
@@ -220,16 +225,18 @@
     blk_dev = table.shape[0]
     n_tiles, per_tile, tsamp, _ = values.shape
     gscale = (tsamp * n_tiles * per_tile / blk_dev) ** (-0.5)
-    owners = block_ids // blk_dev
-    local_index = block_ids % blk_dev
-    matches = owners.reshape(-1)[:, None] == jnp.arange(peers, dtype=jnp.int32)[None, :]
-    wanted = jnp.max(jnp.where(matches, local_index.reshape(-1)[:, None], 0), axis=0)
-    idx = swap(wanted.reshape(peers, 1, 1))
+    ids = block_ids.T
+    owners = ids // blk_dev
+    local_index = (ids % blk_dev).reshape(1, 1, -1)
+    matches = owners.reshape(1, 1, -1) == jnp.arange(peers, dtype=jnp.int32).reshape(peers, 1, 1)
+    wanted = jnp.max(jnp.where(matches, local_index, 0), axis=2, keepdims=True)
+    idx = swap(wanted)
     rows_t = prepare(table, linear, block_class)
-    pulled = swap(pick(idx, rows_t))
+    picked, flat = pick(idx, rows_t)
+    pulled = swap(picked)
     acc, residual = tiles(owners, values, pulled, target, gscale)
     recv = swap(acc)
-    emb_grad, lin_grad = reduce_grads(idx, block_class, recv, rows_t)
+    emb_grad, lin_grad = reduce_grads(flat, block_class, recv, rows_t)
     return emb_grad, lin_grad, residual
 
 

time: 279 us -> 277 us (level)
  no operation moved by 1% of the time
where the time goes in v3:
time: 277 us; the launch traced here: 273 us
  blocking collectives  214 us (77%)
  Pallas kernels  42.1 us (15%)
  starting transfers between devices  10 us (4%)
  local copies, waits for them, and re-layouts  3.85 us (1%)
    all_to_all x2, blocking collectives, swap(): return lax.all_to_all(x, AXES, split_axis=0, concat_axis=0, tiled=True)  214 us
    pallas_call x1, Pallas kernels, tiles(): pl.pallas_call(lambda *refs: tiles_body(gscale, *refs), grid=(n_tiles //...  30.4 us
    all_to_all x1, starting transfers between devices, swap(): return lax.all_to_all(x, AXES, split_axis=0, concat_axis=0, tiled=True)  10 us
    pallas_call x1, Pallas kernels, reduce_grads(): pl.pallas_call(reduce_body, in_specs=[scalars, scalars, whole, whole], ou...  6.31 us
  transfers between devices with their start and end apart: 1, of which 1 were waited for; matrix products, arithmetic and copies ran while one was open for 0% of the time, Pallas kernels for 1%

profile of v3, /device:TPU:66, one launch (start us, length us, event | category | flops | bytes accessed | tf_op | source)
XLA Modules:
  0.0 272.6 jit_solution(5588785745625626757)
XLA Ops:
  0.6 0.7 add_select_fusion.1
  1.3 0.1 broadcast_in_dim.17
  1.4 0.1 eq.25
  1.5 0.1 select_reduce_fusion
  1.6 0.7 copy.10
  2.4 10.0 %all-to-all-start = ((s32[128,1,1]{2,1,0:T(1,128)}), s32[128,1,1]{2,1,0:T(1,128)S(1)}, u32[]{:S(2)}, u32[]{:S(2)}) async-start(s32[128,1,1]{2,1,0:T(1,128)} %copy.10), calls=%async_computation | async-start | bytes 131072 | tf_op jit(solution)/shard_map/all_to_all | solution.py:17
  12.4 0.0 copy-start
  12.4 1.6 copy-done
  14.0 0.0 copy-start.2
  14.0 0.7 copy-done.2
  14.7 0.0 copy-start.3
  14.7 0.7 copy-done.3
  15.3 3.1 %prepare.1.rows_ref = bf16[32,264,128]{2,1,0:T(8,128)(2,1)S(1)} custom-call(s32[32]{0:T(128)S(1)} %copy-done.3, bf16[32,128,256]{2,1,0:T(8,128)(2,1)S(1)} %copy-done, bf16[32,128]{1,0:T(8,128)(2,1)S(1)} %copy-done.2), custom_call_target="tpu_custom_call" | custom-call | flops 16777216 | bytes 4194304 | tf_op jit(solution)/shard_map/prepare/pallas_call | solution.py:46
  18.5 0.7 all-to-all-done.idx_ref
  19.1 2.3 pick.1
  21.5 0.0 copy-start.1
  21.5 107.2 %all_to_all.15.refs_2_ = bf16[128,264,128]{2,1,0:T(8,128)(2,1)S(1)} all-to-all(bf16[128,264,128]{2,1,0:T(8,128)(2,1)S(1)} %get-tuple-element.10), channel_id=1, replica_groups=mesh['group'=4,'member'=32] {'group','member'}, dimensions={0} | all-to-all | bytes 17301504 | tf_op jit(solution)/shard_map/all_to_all | solution.py:17
  128.7 0.0 copy-done.1
  128.7 30.4 %tiles.1 = (bf16[128,264,128]{2,1,0:T(8,128)(2,1)S(1)}, f32[32,128]{1,0:T(8,128)}) custom-call(s32[16,32]{1,0:T(8,128)S(1)} %get-tuple-element.15.refs_0_, bf16[32,16,128,128]{3,2,1,0:T(8,128)(2,1)} %refs_1_.1, bf16[128,264,128]{2,1,0:T(8,128)(2,1)S(1)} %all_to_all.15.refs_2_, f32[32,128]{1,0:T(8,128)S(1)} %copy-done.1), custom_call_target="tpu_custom_call" | custom-call | tf_op jit(solution)/shard_map/tiles/pallas_call | solution.py:148
  159.1 0.0 copy-start.4
  159.1 107.3 %all_to_all.16.recv_ref = bf16[128,264,128]{2,1,0:T(8,128)(2,1)S(1)} all-to-all(bf16[128,264,128]{2,1,0:T(8,128)(2,1)S(1)} %get-tuple-element.11), channel_id=1, replica_groups=mesh['group'=4,'member'=32] {'group','member'}, dimensions={0} | all-to-all | bytes 17301504 | tf_op jit(solution)/shard_map/all_to_all | solution.py:17
  266.3 0.0 copy-done.4
  266.3 6.3 %reduce_grads.1 = (f32[32,128,256]{2,1,0:T(8,128)}, f32[32,128]{1,0:T(8,128)}) custom-call(s32[128]{0:T(128)S(1)} %get-tuple-element.9.idx_ref, s32[32]{0:T(128)S(1)} %copy-done.4, bf16[128,264,128]{2,1,0:T(8,128)(2,1)S(1)} %all_to_all.16.recv_ref, bf16[32,264,128]{2,1,0:T(8,128)(2,1)S(1)} %prepare.1.rows_ref), custom_call_target="tpu_custom_call" | custom-call | tf_op jit(solution)/shard_map/reduce_grads/pallas_call | solution.py:205
Async XLA Ops:
  2.4 16.7 %all-to-all-start = ((s32[128,1,1]{2,1,0:T(1,128)}), s32[128,1,1]{2,1,0:T(1,128)S(1)}, u32[]{:S(2)}, u32[]{:S(2)}) async-start(s32[128,1,1]{2,1,0:T(1,128)} %copy.10), calls=%async_computation | async-start | bytes 131072 | tf_op jit(solution)/shard_map/all_to_all | solution.py:17
  12.4 1.6 copy-start
  14.0 0.7 copy-start.2
  14.7 0.7 copy-start.3
  21.5 107.2 %copy-start.1 = (f32[32,128]{1,0:T(8,128)S(1)}, f32[32,128]{1,0:T(8,128)}, u32[]{:S(2)}) copy-start(f32[32,128]{1,0:T(8,128)} %refs_3_.1) | copy-start | bytes 49156
  159.1 107.3 %copy-start.4 = (s32[32]{0:T(128)S(1)}, s32[32]{0:T(128)}, u32[]{:S(2)}) copy-start(s32[32]{0:T(128)} %cls_ref.3) | copy-start | bytes 388

commit v4 on v3

--- a/solution.py
+++ b/solution.py
@@ -87,7 +87,7 @@
 
     @pl.when(step == 0)
     def _():
-        @pl.loop(0, peers)
+        @pl.loop(0, peers, unroll=4)
         def _(o):
             acc_ref[o] = jnp.zeros((rows, brows), F32)
 
@@ -133,7 +133,7 @@
 
     @pl.when(step == pl.num_programs(0) - 1)
     def _():
-        @pl.loop(0, peers)
+        @pl.loop(0, peers, unroll=4)
         def _(o):
             extra = acc_ref[o, cols:]
             hi = extra.astype(BF16).astype(F32)
@@ -173,18 +173,18 @@
     blocks, rows, brows = acc_ref.shape
     cols = rows - EXTRA
 
-    @pl.loop(0, blocks)
+    @pl.loop(0, blocks, unroll=4)
     def _(j):
         acc_ref[j] = jnp.zeros((rows, brows), F32)
 
-    @pl.loop(0, peers, unroll=2)
+    @pl.loop(0, peers, unroll=4)
     def _(p):
         j = idx_ref[p]
         acc_ref[j] += recv_ref[p].astype(F32)
 
     row = lax.broadcasted_iota(jnp.int32, (cols, brows), 0)
 
-    @pl.loop(0, blocks, unroll=2)
+    @pl.loop(0, blocks, unroll=4)
     def _(j):
         extra = acc_ref[j, cols:]
         lin_ref[pl.ds(j, 1), :] = extra[0:1] + extra[2:3]

time: 277 us -> 275 us (level)
  no operation moved by 1% of the time
where the time goes in v4:
time: 275 us; the launch traced here: 271 us
  blocking collectives  214 us (78%)
  Pallas kernels  40.1 us (15%)
  starting transfers between devices  10 us (4%)
  local copies, waits for them, and re-layouts  3.85 us (1%)
    all_to_all x2, blocking collectives, swap(): return lax.all_to_all(x, AXES, split_axis=0, concat_axis=0, tiled=True)  214 us
    pallas_call x1, Pallas kernels, tiles(): pl.pallas_call(lambda *refs: tiles_body(gscale, *refs), grid=(n_tiles //...  29.2 us
    all_to_all x1, starting transfers between devices, swap(): return lax.all_to_all(x, AXES, split_axis=0, concat_axis=0, tiled=True)  10 us
  transfers between devices with their start and end apart: 1, of which 1 were waited for; matrix products, arithmetic and copies ran while one was open for 0% of the time, Pallas kernels for 1%

profile of v4, /device:TPU:66, one launch (start us, length us, event | category | flops | bytes accessed | tf_op | source)
XLA Modules:
  0.0 270.6 jit_solution(3313359089591344317)
XLA Ops:
  0.6 0.7 add_select_fusion.1
  1.3 0.1 broadcast_in_dim.17
  1.4 0.1 eq.25
  1.5 0.1 select_reduce_fusion
  1.6 0.7 copy.10
  2.4 10.0 %all-to-all-start = ((s32[128,1,1]{2,1,0:T(1,128)}), s32[128,1,1]{2,1,0:T(1,128)S(1)}, u32[]{:S(2)}, u32[]{:S(2)}) async-start(s32[128,1,1]{2,1,0:T(1,128)} %copy.10), calls=%async_computation | async-start | bytes 131072 | tf_op jit(solution)/shard_map/all_to_all | solution.py:17
  12.4 0.0 copy-start
  12.4 1.6 copy-done
  14.0 0.0 copy-start.2
  14.0 0.7 copy-done.2
  14.7 0.0 copy-start.3
  14.7 0.7 copy-done.3
  15.3 3.1 %prepare.1.rows_ref = bf16[32,264,128]{2,1,0:T(8,128)(2,1)S(1)} custom-call(s32[32]{0:T(128)S(1)} %copy-done.3, bf16[32,128,256]{2,1,0:T(8,128)(2,1)S(1)} %copy-done, bf16[32,128]{1,0:T(8,128)(2,1)S(1)} %copy-done.2), custom_call_target="tpu_custom_call" | custom-call | flops 16777216 | bytes 4194304 | tf_op jit(solution)/shard_map/prepare/pallas_call | solution.py:46
  18.5 0.7 all-to-all-done.idx_ref
  19.1 2.3 pick.1
  21.5 0.0 copy-start.1
  21.5 107.2 %all_to_all.15.refs_2_ = bf16[128,264,128]{2,1,0:T(8,128)(2,1)S(1)} all-to-all(bf16[128,264,128]{2,1,0:T(8,128)(2,1)S(1)} %get-tuple-element.10), channel_id=1, replica_groups=mesh['group'=4,'member'=32] {'group','member'}, dimensions={0} | all-to-all | bytes 17301504 | tf_op jit(solution)/shard_map/all_to_all | solution.py:17
  128.7 0.0 copy-done.1
  128.7 29.2 %tiles.1 = (bf16[128,264,128]{2,1,0:T(8,128)(2,1)S(1)}, f32[32,128]{1,0:T(8,128)}) custom-call(s32[16,32]{1,0:T(8,128)S(1)} %get-tuple-element.15.refs_0_, bf16[32,16,128,128]{3,2,1,0:T(8,128)(2,1)} %refs_1_.1, bf16[128,264,128]{2,1,0:T(8,128)(2,1)S(1)} %all_to_all.15.refs_2_, f32[32,128]{1,0:T(8,128)S(1)} %copy-done.1), custom_call_target="tpu_custom_call" | custom-call | tf_op jit(solution)/shard_map/tiles/pallas_call | solution.py:148
  157.9 0.0 copy-start.4
  157.9 107.2 %all_to_all.16.recv_ref = bf16[128,264,128]{2,1,0:T(8,128)(2,1)S(1)} all-to-all(bf16[128,264,128]{2,1,0:T(8,128)(2,1)S(1)} %get-tuple-element.11), channel_id=1, replica_groups=mesh['group'=4,'member'=32] {'group','member'}, dimensions={0} | all-to-all | bytes 17301504 | tf_op jit(solution)/shard_map/all_to_all | solution.py:17
  265.1 0.0 copy-done.4
  265.1 5.5 %reduce_grads.1 = (f32[32,128,256]{2,1,0:T(8,128)}, f32[32,128]{1,0:T(8,128)}) custom-call(s32[128]{0:T(128)S(1)} %get-tuple-element.9.idx_ref, s32[32]{0:T(128)S(1)} %copy-done.4, bf16[128,264,128]{2,1,0:T(8,128)(2,1)S(1)} %all_to_all.16.recv_ref, bf16[32,264,128]{2,1,0:T(8,128)(2,1)S(1)} %prepare.1.rows_ref), custom_call_target="tpu_custom_call" | custom-call | tf_op jit(solution)/shard_map/reduce_grads/pallas_call | solution.py:205
Async XLA Ops:
  2.4 16.7 %all-to-all-start = ((s32[128,1,1]{2,1,0:T(1,128)}), s32[128,1,1]{2,1,0:T(1,128)S(1)}, u32[]{:S(2)}, u32[]{:S(2)}) async-start(s32[128,1,1]{2,1,0:T(1,128)} %copy.10), calls=%async_computation | async-start | bytes 131072 | tf_op jit(solution)/shard_map/all_to_all | solution.py:17
  12.4 1.6 copy-start
  14.0 0.7 copy-start.2
  14.7 0.7 copy-start.3
  21.5 107.2 %copy-start.1 = (f32[32,128]{1,0:T(8,128)S(1)}, f32[32,128]{1,0:T(8,128)}, u32[]{:S(2)}) copy-start(f32[32,128]{1,0:T(8,128)} %refs_3_.1) | copy-start | bytes 49156
  157.9 107.2 %copy-start.4 = (s32[32]{0:T(128)S(1)}, s32[32]{0:T(128)}, u32[]{:S(2)}) copy-start(s32[32]{0:T(128)} %cls_ref.3) | copy-start | bytes 388
